TPU v7x, 32 devices: a whole 2x2x4 slice. The times are simulated.
32 devices in a mesh: groups: 2 (over x), tile: 16 (over z, y, core).
Axes of the slice: x: 2, y: 2, z: 4, core: 2. Of those that a mesh axis runs over, the one named last changes fastest.
Arguments:
- queries: bfloat16 [8, 768, 2560], P('groups', 'tile'), parts along dimension 0, may hold values from -60 to 60
- frame_kv: bfloat16 [8, 768, 2, 2560], P('groups', 'tile'), parts along dimension 0, may hold values from -7 to 7
- memory_kv: bfloat16 [8, 768, 2, 2560], P('groups', 'tile'), parts along dimension 0, may hold values from -6 to 6
- window_offsets: int32 [10], P('groups'), parts along dimension 0, may hold values from -3 to 3, as said below
- memory_frame: int32 [96, 5], P(('groups', 'tile')), parts along dimension 0, may hold values from 0 to 3
- memory_tile: int32 [96, 5], P(('groups', 'tile')), parts along dimension 0, may hold values from 0 to 47, as said below
Outputs:
- attended: bfloat16 [8, 768, 2560], P('groups', 'tile'), parts along dimension 0
There are 2 independent parts, one for each index of `groups`. A program takes and returns all parts, laid end to end along the dimension named above; each array names one. Nothing has to cross between parts.
Inputs may be any that keep to these rules, and one draw needn't show every extreme that they name: `window_offsets`: the values are distinct and include -3, 0 and 3. `memory_tile`: for every device d, the 15 entries of rows d * 3 to d * 3 + 2 name tiles t whose values t // 3 are all different.
All inputs are finite; a program needn't handle non-finite values.
Results may differ from a plain program's by a relative error of at most 0.0033.
Values may be sent and summed in bfloat16 or wider, within the bound.
A program may use at most 256 MiB of HBM per device.

v0:
```python
import jax
import jax.numpy as jnp
from jax import lax
from jax.sharding import PartitionSpec as P

HEAD_DIM = 128
TILE_TOK = 16
TPD = 3
RADIUS = 3


def with_halo(array, sides, width):
    for axis, dim in sides:
        size, length = (lax.axis_size(axis), array.shape[dim])
        up = [(i, (i + 1) % size) for i in range(size - 1)]
        down = [(j, i) for i, j in up]
        last = lax.slice_in_dim(array, length - width, length, axis=dim)
        leading = lax.slice_in_dim(array, 0, width, axis=dim)
        before = lax.ppermute(last, axis, up)
        after = lax.ppermute(leading, axis, down)
        array = jnp.concatenate([before, array, after], axis=dim)
    return array


def body(queries, frame_kv, memory_kv, window_offsets, memory_frame, memory_tile):
    video_moments = frame_kv.shape[0]
    columns = frame_kv.shape[3]
    list_length = memory_tile.shape[1]
    stored_frames = memory_kv.shape[0]
    peer_count = lax.axis_size("tile")
    device_index = lax.axis_index("tile")
    span_tiles = TPD + 2 * RADIUS
    extended = with_halo(frame_kv, (("tile", 1),), RADIUS * TILE_TOK)
    ext_tiles = extended.reshape(video_moments, span_tiles, TILE_TOK, 2, columns)
    local_ids = jnp.arange(TPD, dtype=jnp.int32)
    span_ids = jnp.arange(span_tiles, dtype=jnp.int32)
    offset_grid = span_ids[None, :] - local_ids[:, None] - RADIUS
    in_window = jnp.any(offset_grid[:, :, None] == window_offsets[None, None, :], axis=2)
    global_tiles = device_index * TPD + span_ids - RADIUS
    inside = (global_tiles >= 0) & (global_tiles < peer_count * TPD)
    usable = in_window & inside[None, :]
    usable_mask = usable[:, None, None, None, None, :, None]
    owners = memory_tile // TPD
    wanted = memory_frame * TPD + memory_tile % TPD
    outgoing = jnp.full((peer_count,), -1, jnp.int32).at[owners.reshape(-1)].set(wanted.reshape(-1))
    requested = lax.all_to_all(
        outgoing.reshape(peer_count, 1), "tile", split_axis=0, concat_axis=0, tiled=True
    ).reshape(peer_count)
    memory_store = memory_kv.reshape(stored_frames * TPD, TILE_TOK, 2, columns)
    picked = memory_store[jnp.clip(requested, 0, stored_frames * TPD - 1)]
    fetched = lax.all_to_all(picked, "tile", split_axis=0, concat_axis=0, tiled=True)
    memory_keys = fetched[owners.reshape(-1)].reshape(TPD, list_length * TILE_TOK, 2, columns)
    query_rows = queries.reshape(video_moments, TPD, TILE_TOK, columns)
    group_span = columns // 4
    group_heads = group_span // HEAD_DIM
    score_scale = HEAD_DIM ** (-0.5)
    outputs = []
    for group_index in range(4):
        low = group_index * group_span
        high = low + group_span
        query_part = query_rows[..., low:high].reshape(
            video_moments, TPD, TILE_TOK, group_heads, HEAD_DIM
        )
        near_keys = ext_tiles[..., 0, low:high].reshape(
            video_moments, span_tiles, TILE_TOK, group_heads, HEAD_DIM
        )
        near_values = ext_tiles[..., 1, low:high].reshape(
            video_moments, span_tiles, TILE_TOK, group_heads, HEAD_DIM
        )
        far_keys = memory_keys[:, :, 0, low:high].reshape(TPD, -1, group_heads, HEAD_DIM)
        far_values = memory_keys[:, :, 1, low:high].reshape(TPD, -1, group_heads, HEAD_DIM)
        near_scores = (
            jnp.einsum(
                "fathd,gskhd->ahftgsk", query_part, near_keys, preferred_element_type=jnp.float32
            )
            * score_scale
        )
        near_scores = jnp.where(usable_mask, near_scores, -1e30)
        far_scores = (
            jnp.einsum(
                "fathd,amhd->ahftm", query_part, far_keys, preferred_element_type=jnp.float32
            )
            * score_scale
        )
        near_top = jnp.max(near_scores, axis=(4, 5, 6))
        far_top = jnp.max(far_scores, axis=4)
        row_top = jnp.maximum(near_top, far_top)
        near_terms = jnp.exp(near_scores - row_top[..., None, None, None])
        far_terms = jnp.exp(far_scores - row_top[..., None])
        row_total = jnp.sum(near_terms, axis=(4, 5, 6)) + jnp.sum(far_terms, axis=4)
        near_weights = near_terms.astype(jnp.bfloat16)
        far_weights = far_terms.astype(jnp.bfloat16)
        summed = jnp.einsum(
            "ahftgsk,gskhd->fathd", near_weights, near_values, preferred_element_type=jnp.float32
        )
        summed = summed + jnp.einsum(
            "ahftm,amhd->fathd", far_weights, far_values, preferred_element_type=jnp.float32
        )
        attended = summed / jnp.transpose(row_total, (2, 0, 3, 1))[..., None]
        outputs.append(
            attended.astype(jnp.bfloat16).reshape(video_moments, TPD * TILE_TOK, group_span)
        )
    return jnp.concatenate(outputs, axis=2)


def solution(mesh):
    in_specs = (
        P("groups", "tile", None),
        P("groups", "tile", None, None),
        P("groups", "tile", None, None),
        P("groups"),
        P(("groups", "tile"), None),
        P(("groups", "tile"), None),
    )
    out_specs = P("groups", "tile", None)
    return jax.shard_map(body, mesh=mesh, in_specs=in_specs, out_specs=out_specs, check_vma=False)
```

profile of v0, /device:TPU:0, one launch (start us, length us, event | category | flops | bytes accessed | tf_op | source)
XLA Modules:
  0.0 274.6 jit_solution(7747917935762710504)
XLA Ops:
  0.0 3.8 %collective-permute-start = (bf16[4,48,2,2560]{3,2,1,0:T(2,128)(2,1)}, bf16[4,48,2,2560]{3,2,1,0:T(2,128)(2,1)}, u32[]{:S(2)}, u32[]{:S(2)}) collective-permute-start(bf16[4,48,2,2560]{3,2,1,0:T(2,128)(2,1)} %param.7), channel_id=1, source_target_pairs={{0,1},{1,2},{2,3},{3,4},{4,5},{5,6},{6,7},{7,8},{8,9},{9,10},{10,1... | collective-permute-start | bytes 5898248 | tf_op jit(solution)/shard_map/ppermute | solution.py:19
  7.3 8.0 %all-to-all-start = ((s32[16,1,1]{2,1,0:T(1,128)}), s32[16,1,1]{2,1,0:T(1,128)S(1)}, u32[]{:S(2)}, u32[]{:S(2)}) async-start(s32[16,1,1]{2,1,0:T(1,128)} %copy.318), calls=%async_computation | async-start | bytes 16384 | tf_op jit(solution)/shard_map/all_to_all | solution.py:46
  21.8 12.8 %all-to-all-done = s32[16,1,1]{2,1,0:T(1,128)S(1)} async-done(((s32[16,1,1]{2,1,0:T(1,128)}), s32[16,1,1]{2,1,0:T(1,128)S(1)}, u32[]{:S(2)}, u32[]{:S(2)}) %all-to-all-start) | async-done | bytes 96 | tf_op jit(solution)/shard_map/all_to_all | solution.py:46
  35.0 7.0 %gather_fusion = bf16[16,16,2,2560]{3,2,1,0:T(2,128)(2,1)} fusion(bf16[12,16,2,2560]{3,2,1,0:T(2,128)(2,1)S(1)} %bitcast.208, s32[1024]{0:T(1024)S(1)} %pad_clamp_fusion.1), kind=kCustom, calls=%fused_computation | custom fusion | bytes 5242944 | tf_op jit(solution)/shard_map/gather | solution.py:50
  41.9 20.9 %all-to-all-start.1 = ((bf16[16,16,2,2560]{3,2,1,0:T(2,128)(2,1)}), bf16[16,16,2,2560]{3,2,1,0:T(2,128)(2,1)}, u32[]{:S(2)}, u32[]{:S(2)}) async-start(bf16[16,16,2,2560]{3,2,1,0:T(2,128)(2,1)} %gather_fusion), calls=%async_computation.1 | async-start | bytes 5242880 | tf_op jit(solution)/shard_map/all_to_all | solution.py:51
  62.9 11.4 %pad_maximum_fusion = bf16[4,144,2,2560]{3,2,1,0:T(2,128)(2,1)S(1)} fusion(bf16[4,48,2,2560]{3,2,1,0:T(2,128)(2,1)} %collective-permute-done.1, bf16[4,48,2,2560]{3,2,1,0:T(2,128)(2,1)S(1)} %copy-done.12, bf16[4,48,2,2560]{3,2,1,0:T(2,128)(2,1)} %collective-permute-done), kind=kLoop, calls=%fused_computation.31 | loop fusion | flops 5898240 | bytes 11796480 | tf_op jit(solution)/shard_map/concatenate | solution.py:21
  74.3 9.6 %fusion.98 = (bf16[4,9,16,1,640]{4,3,2,1,0:T(2,128)(2,1)S(1)}, bf16[4,9,16,1,640]{4,3,2,1,0:T(2,128)(2,1)}, bf16[4,9,16,1,640]{4,3,2,1,0:T(2,128)(2,1)}, bf16[4,...) fusion(bf16[4,9,16,2,2560]{4,3,2,1,0:T(2,128)(2,1)S(1)} %bitcas, ...), kind=kLoop, calls=%fused_computation.136 | loop fusion | bytes 11796480 | tf_op jit(solution)/shard_map/slice | solution.py:67
  84.8 2.7 reshape_squeeze.48
  89.9 2.7 reshape_squeeze.60
  94.9 2.7 reshape_squeeze.57
  99.9 2.7 reshape_squeeze.56
  104.9 2.7 reshape_squeeze.53
  109.9 2.7 reshape_squeeze.52
  116.4 2.8 %reshape_squeeze.61 = bf16[4,9,16,5,128]{4,3,2,1,0:T(8,128)(2,1)} reshape(bf16[4,9,16,1,640]{4,2,1,0,3:T(8,128)(2,1)} %copy.455) | data formatting | bytes 1474560 | tf_op jit(solution)/shard_map/reshape;squeeze | solution.py:64
  119.3 10.0 %fusion.48 = f32[5,4,9,16,4,3,16]{6,3,5,4,2,1,0:T(8,128)} fusion(bf16[4,9,16,5,128,1,1]{4,3,2,1,0,6,5:T(8,128)(2,1)} %bitcast.218, bf16[4,3,16,5,128,1,1]{4,3,2,1,0,6,5:T(8,128)(2,1)} %bitcast.221), kind=kOutput, calls=%fused_computation.61 | convolution fusion | flops 141557760 | bytes 3194880 | tf_op jit(solution)/shard_map/fathd,gskhd->ahftgsk/dot_general | solution.py:73
  129.3 8.5 %fusion.51 = f32[5,4,9,16,4,3,16]{6,3,5,4,2,1,0:T(8,128)} fusion(bf16[4,9,16,5,128,1,1]{4,3,2,1,0,6,5:T(8,128)(2,1)S(1)} %bitcast.216, bf16[4,3,16,5,128,1,1]{4,3,2,1,0,6,5:T(8,128)(2,1)S(1)} %bitcast.220), kind=kOutput, calls=%fused_computation.64 | convolution fusion | flops 141557760 | bytes 3194880 | tf_op jit(solution)/shard_map/fathd,gskhd->ahftgsk/dot_general | solution.py:73
  137.8 8.4 %fusion.8 = (f32[3,5,4,16]{3,0,2,1:T(4,128)}, f32[5,4,9,16,4,3,16]{6,3,5,4,2,1,0:T(8,128)}) fusion(pred[3,9]{0,1:T(8,128)(4,1)S(1)} %copy.314, bf16[4,3,16,5,128,1,1]{4,3,2,1,0,6,5:T(8,128)(2,1)S(1)} %bitcast.222, bf16[4,9,16,5,128,1,1]{4,3,2,1,0,6,5:T(8,128)(2,1)S(1)} %bitcast.217), kind=kOutput, calls=%fused_computation.19 | convolution fusion | flops 143215680 | bytes 3198747 | tf_op jit(solution)/shard_map/fathd,gskhd->ahftgsk/dot_general | solution.py:73
  146.1 8.9 %gather_fusion.1 = bf16[15,16,2,2560]{3,2,1,0:T(2,128)(2,1)} fusion(bf16[16,16,2,2560]{3,2,1,0:T(2,128)(2,1)} %all-to-all-done.1, s32[1024]{0:T(1024)S(1)} %pad_clamp_fusion), kind=kCustom, calls=%fused_computation.1 | custom fusion | bytes 4915260 | tf_op jit(solution)/shard_map/gather | solution.py:52
  182.2 32.5 %fusion = (f32[3,5,4,16]{3,0,2,1:T(4,128)S(1)}, f32[3,5,4,16]{3,0,2,1:T(4,128)S(1)}, f32[3,5,4,16]{3,0,2,1:T(4,128)S(1)}, f32[3,5,4,16]{3,0,2,1:T(4,128)S(1)}, b...) fusion(f32[5,4,9,16,4,3,16]{6,3,5,4,2,1,0:T(8,128)} %get-tuple-element.51, ...), kind=kOutput, calls=%fused_computation.11 | convolution fusion | flops 149295360 | bytes 10955547 | tf_op jit(solution)/shard_map/fathd,gskhd->ahftgsk/dot_general | solution.py:73
  218.2 28.4 %fusion.2 = (f32[3,5,4,16]{3,0,2,1:T(4,128)S(1)}, f32[3,5,4,16]{3,0,2,1:T(4,128)S(1)}, f32[3,5,4,16]{3,0,2,1:T(4,128)S(1)}, bf16[3,5,4,16,4,9,16]{3,6,0,2,5,4,1:...) fusion(f32[5,4,9,16,4,3,16]{6,3,5,4,2,1,0:T(8,128)} %get-tuple-element.52, ...), kind=kLoop, calls=%fused_computation.13 | loop fusion | flops 8291520 | bytes 9976347 | tf_op jit(solution)/shard_map/reduce_sum | solution.py:90
  246.7 2.5 fusion.29
  250.0 6.1 %fusion.26 = f32[4,3,16,5,128]{4,2,0,1,3:T(8,128)S(1)} fusion(bf16[3,5,4,16,4,9,16]{3,6,0,2,5,4,1:T(8,128)(2,1)} %get-tuple-element.14, bf16[4,9,16,5,128,1,1]{4,3,2,1,0,6,5:T(8,128)(2,1)S(1)} %bitcast.213), kind=kOutput, calls=%fused_computation.34 | convolution fusion | flops 141557760 | bytes 2334720 | tf_op jit(solution)/shard_map/ahftgsk,gskhd->fathd/dot_general | solution.py:93
  257.5 6.1 %fusion.23 = f32[4,3,16,5,128]{4,2,0,1,3:T(8,128)S(1)} fusion(bf16[3,5,4,16,4,9,16]{3,6,0,2,5,4,1:T(8,128)(2,1)} %get-tuple-element.13, bf16[4,9,16,5,128,1,1]{4,3,2,1,0,6,5:T(8,128)(2,1)S(1)} %bitcast.212), kind=kOutput, calls=%fused_computation.33 | convolution fusion | flops 141557760 | bytes 2334720 | tf_op jit(solution)/shard_map/ahftgsk,gskhd->fathd/dot_general | solution.py:93
  265.1 6.1 %fusion.20 = f32[4,3,16,5,128]{4,2,0,1,3:T(8,128)S(1)} fusion(bf16[3,5,4,16,4,9,16]{3,6,0,2,5,4,1:T(8,128)(2,1)} %get-tuple-element.12, bf16[4,9,16,5,128,1,1]{4,3,2,1,0,6,5:T(8,128)(2,1)S(1)} %bitcast.211), kind=kOutput, calls=%fused_computation.32 | convolution fusion | flops 141557760 | bytes 2334720 | tf_op jit(solution)/shard_map/ahftgsk,gskhd->fathd/dot_general | solution.py:93
  (125 shorter events, 63.8 us)
Async XLA Ops:
  0.0 35.0 %copy-start = (bf16[4,48,2,2560]{3,2,1,0:T(2,128)(2,1)S(1)}, bf16[4,48,2,2560]{3,2,1,0:T(2,128)(2,1)}, u32[]{:S(2)}) copy-start(bf16[4,48,2,2560]{3,2,1,0:T(2,128)(2,1)} %param.8) | copy-start | bytes 5898244
  0.0 62.8 %collective-permute-start = (bf16[4,48,2,2560]{3,2,1,0:T(2,128)(2,1)}, bf16[4,48,2,2560]{3,2,1,0:T(2,128)(2,1)}, u32[]{:S(2)}, u32[]{:S(2)}) collective-permute-start(bf16[4,48,2,2560]{3,2,1,0:T(2,128)(2,1)} %param.7), channel_id=1, source_target_pairs={{0,1},{1,2},{2,3},{3,4},{4,5},{5,6},{6,7},{7,8},{8,9},{9,10},{10,1... | collective-permute-start | bytes 5898248 | tf_op jit(solution)/shard_map/ppermute | solution.py:19
  3.8 59.1 %collective-permute-start.1 = (bf16[4,48,2,2560]{3,2,1,0:T(2,128)(2,1)}, bf16[4,48,2,2560]{3,2,1,0:T(2,128)(2,1)}, u32[]{:S(2)}, u32[]{:S(2)}) collective-permute-start(bf16[4,48,2,2560]{3,2,1,0:T(2,128)(2,1)} %param.7), channel_id=1, source_target_pairs={{1,0},{2,1},{3,2},{4,3},{5,4},{6,5},{7,6},{8,7},{9,8},{10,9},{11,1... | collective-permute-start | bytes 5898248 | tf_op jit(solution)/shard_map/ppermute | solution.py:20
  7.3 27.3 %all-to-all-start = ((s32[16,1,1]{2,1,0:T(1,128)}), s32[16,1,1]{2,1,0:T(1,128)S(1)}, u32[]{:S(2)}, u32[]{:S(2)}) async-start(s32[16,1,1]{2,1,0:T(1,128)} %copy.318), calls=%async_computation | async-start | bytes 16384 | tf_op jit(solution)/shard_map/all_to_all | solution.py:46
  41.9 20.9 %copy-start.12 = (bf16[4,48,2,2560]{3,2,1,0:T(2,128)(2,1)S(1)}, bf16[4,48,2,2560]{3,2,1,0:T(2,128)(2,1)}, u32[]{:S(2)}) copy-start(bf16[4,48,2,2560]{3,2,1,0:T(2,128)(2,1)} %param.7) | copy-start | bytes 5898244
  41.9 104.2 %all-to-all-start.1 = ((bf16[16,16,2,2560]{3,2,1,0:T(2,128)(2,1)}), bf16[16,16,2,2560]{3,2,1,0:T(2,128)(2,1)}, u32[]{:S(2)}, u32[]{:S(2)}) async-start(bf16[16,16,2,2560]{3,2,1,0:T(2,128)(2,1)} %gather_fusion), calls=%async_computation.1 | async-start | bytes 5242880 | tf_op jit(solution)/shard_map/all_to_all | solution.py:51
  119.3 10.0 %copy-start.7 = (bf16[4,9,16,5,128]{4,3,2,1,0:T(8,128)(2,1)S(1)}, bf16[4,9,16,5,128]{4,3,2,1,0:T(8,128)(2,1)}, u32[]{:S(2)}) copy-start(bf16[4,9,16,5,128]{4,3,2,1,0:T(8,128)(2,1)} %reshape_squeeze.57) | copy-start | bytes 2211844
  119.3 10.0 %copy-start.9 = (bf16[4,3,16,5,128]{4,3,2,1,0:T(8,128)(2,1)S(1)}, bf16[4,3,16,5,128]{4,3,2,1,0:T(8,128)(2,1)}, u32[]{:S(2)}) copy-start(bf16[4,3,16,5,128]{4,3,2,1,0:T(8,128)(2,1)} %reshape.187) | copy-start | bytes 737284
  129.3 8.5 %copy-start.11 = (bf16[4,3,16,5,128]{4,3,2,1,0:T(8,128)(2,1)S(1)}, bf16[4,3,16,5,128]{4,3,2,1,0:T(8,128)(2,1)}, u32[]{:S(2)}) copy-start(bf16[4,3,16,5,128]{4,3,2,1,0:T(8,128)(2,1)} %reshape.179) | copy-start | bytes 737284
  155.0 7.9 %copy-start.10 = (bf16[4,3,16,5,128]{4,3,2,1,0:T(8,128)(2,1)S(1)}, bf16[4,3,16,5,128]{4,3,2,1,0:T(8,128)(2,1)}, u32[]{:S(2)}) copy-start(bf16[4,3,16,5,128]{4,3,2,1,0:T(8,128)(2,1)} %reshape.189) | copy-start | bytes 737284
  158.4 20.6 %copy-start.20 = (f32[3,5,4,16]{3,0,2,1:T(4,128)S(1)}, f32[3,5,4,16]{3,0,2,1:T(4,128)}, u32[]{:S(2)}) copy-start(f32[3,5,4,16]{3,0,2,1:T(4,128)} %get-tuple-element.50) | copy-start | bytes 11524
  158.4 21.6 %copy-start.8 = (bf16[4,3,16,5,128]{4,3,2,1,0:T(8,128)(2,1)S(1)}, bf16[4,3,16,5,128]{4,3,2,1,0:T(8,128)(2,1)}, u32[]{:S(2)}) copy-start(bf16[4,3,16,5,128]{4,3,2,1,0:T(8,128)(2,1)} %reshape.185) | copy-start | bytes 737284
  158.4 23.7 %copy-start.6 = (bf16[4,9,16,5,128]{4,3,2,1,0:T(8,128)(2,1)S(1)}, bf16[4,9,16,5,128]{4,3,2,1,0:T(8,128)(2,1)}, u32[]{:S(2)}) copy-start(bf16[4,9,16,5,128]{4,3,2,1,0:T(8,128)(2,1)} %reshape_squeeze.53) | copy-start | bytes 2211844
  182.2 34.6 %copy-start.21 = (f32[3,5,4,16]{3,2,1,0:T(4,128)S(1)}, f32[3,5,4,16]{3,2,1,0:T(4,128)}, u32[]{:S(2)}) copy-start(f32[3,5,4,16]{3,2,1,0:T(4,128)} %get-tuple-element.55) | copy-start | bytes 11524
  182.2 34.6 %copy-start.13 = (f32[3,5,4,16,80]{4,3,2,1,0:T(8,128)S(1)}, f32[3,5,4,16,80]{4,3,2,1,0:T(8,128)}, u32[]{:S(2)}) copy-start(f32[3,5,4,16,80]{4,3,2,1,0:T(8,128)} %get-tuple-element.54) | copy-start | bytes 921604
  218.2 28.5 %copy-start.5 = (bf16[4,9,16,5,128]{4,3,2,1,0:T(8,128)(2,1)S(1)}, bf16[4,9,16,5,128]{4,3,2,1,0:T(8,128)(2,1)}, u32[]{:S(2)}) copy-start(bf16[4,9,16,5,128]{4,3,2,1,0:T(8,128)(2,1)} %reshape_squeeze.60) | copy-start | bytes 2211844
  249.9 6.1 %copy-start.16 = (bf16[3,80,5,128]{3,2,1,0:T(8,128)(2,1)S(1)}, bf16[3,80,5,128]{3,2,1,0:T(8,128)(2,1)}, u32[]{:S(2)}) copy-start(bf16[3,80,5,128]{3,2,1,0:T(8,128)(2,1)} %reshape_squeeze.59) | copy-start | bytes 921604
  249.9 6.1 %copy-start.19 = (bf16[3,5,4,16,80]{4,3,2,1,0:T(8,128)(2,1)S(1)}, bf16[3,5,4,16,80]{4,3,2,1,0:T(8,128)(2,1)}, u32[]{:S(2)}) copy-start(bf16[3,5,4,16,80]{4,3,2,1,0:T(8,128)(2,1)} %get-tuple-element.41) | copy-start | bytes 460804
  250.0 7.6 %copy-start.3 = (bf16[4,9,16,5,128]{4,3,2,1,0:T(8,128)(2,1)S(1)}, bf16[4,9,16,5,128]{4,3,2,1,0:T(8,128)(2,1)}, u32[]{:S(2)}) copy-start(bf16[4,9,16,5,128]{4,3,2,1,0:T(8,128)(2,1)} %reshape_squeeze.52) | copy-start | bytes 2211844
  257.5 7.6 %copy-start.2 = (bf16[4,9,16,5,128]{4,3,2,1,0:T(8,128)(2,1)S(1)}, bf16[4,9,16,5,128]{4,3,2,1,0:T(8,128)(2,1)}, u32[]{:S(2)}) copy-start(bf16[4,9,16,5,128]{4,3,2,1,0:T(8,128)(2,1)} %reshape_squeeze.48) | copy-start | bytes 2211844
  265.1 6.2 %copy-start.14 = (bf16[3,80,5,128]{3,2,1,0:T(8,128)(2,1)S(1)}, bf16[3,80,5,128]{3,2,1,0:T(8,128)(2,1)}, u32[]{:S(2)}) copy-start(bf16[3,80,5,128]{3,2,1,0:T(8,128)(2,1)} %reshape_squeeze.51) | copy-start | bytes 921604
  265.1 6.2 %copy-start.18 = (bf16[3,5,4,16,80]{4,3,2,1,0:T(8,128)(2,1)S(1)}, bf16[3,5,4,16,80]{4,3,2,1,0:T(8,128)(2,1)}, u32[]{:S(2)}) copy-start(bf16[3,5,4,16,80]{4,3,2,1,0:T(8,128)(2,1)} %get-tuple-element.37) | copy-start | bytes 460804
  265.1 6.2 %copy-start.22 = (f32[4,3,16,5]{2,0,1,3:T(4,128)S(1)}, f32[4,3,16,5]{2,0,1,3:T(4,128)}, u32[]{:S(2)}) copy-start(f32[4,3,16,5]{2,0,1,3:T(4,128)} %copy.329) | copy-start | bytes 11524
  265.1 9.0 %copy-start.1 = (bf16[4,48,2,2560]{3,2,1,0:T(2,128)(2,1)S(1)}, bf16[4,48,2,2560]{3,2,1,0:T(2,128)(2,1)}, u32[]{:S(2)}) copy-start(bf16[4,48,2,2560]{3,2,1,0:T(2,128)(2,1)} %param.8) | copy-start | bytes 5898244
  (3 other events, 11.8 us)
where the time goes:
time: 280 us; the launch traced here: 275 us
  local copies, waits for them, and re-layouts  90.5 us (32%)
  matrix products  88.8 us (32%)
  other arithmetic  47.5 us (17%)
  starting transfers between devices  33.9 us (12%)
  waiting for transfers between devices  12.8 us (5%)
    dot_general x4, matrix products, body(): jnp.einsum('fathd,gskhd->ahftgsk', query_part, near_keys, preferred_eleme...  59.3 us
    reduce_sum x5, other arithmetic, body(): row_total = jnp.sum(near_terms, axis=(4, 5, 6)) + jnp.sum(far_terms, axis=4)  32 us
    all_to_all x1, starting transfers between devices, body(): lax.all_to_all(picked, 'tile', split_axis=0, concat_axis=0, tiled=True)  20.9 us
    dot_general x4, matrix products, body(): jnp.einsum('ahftgsk,gskhd->fathd', near_weights, near_values, preferred_e...  20.8 us
    unnamed x54, local copies, waits for them, and re-layouts  14.7 us
    all_to_all x1, waiting for transfers between devices, body(): lax.all_to_all(outgoing.reshape(peer_count, 1), 'tile', split_axis=0, con...  12.8 us
    concatenate x1, other arithmetic, with_halo(): array = jnp.concatenate([before, array, after], axis=dim)  11.4 us
    gather x2, local copies, waits for them, and re-layouts, body(): fetched[owners.reshape(-1)].reshape(TPD, list_length * TILE_TOK, 2, columns)  11 us
  transfers between devices with their start and end apart: 4, of which 1 were waited for; matrix products, arithmetic and copies ran while one was open for 36% of the time, Pallas kernels for 0%

commit v1 on v0

v1 whole, which is shorter than its diff:
```python
import functools

import jax
import jax.numpy as jnp
from jax import lax
from jax.experimental import pallas as pl
from jax.experimental.pallas import tpu as pltpu
from jax.sharding import PartitionSpec as P

HEAD_DIM = 128
TILE_TOK = 16
TPD = 3
RADIUS = 3
CHUNKS = 5
OFF = -1e30


def kernel(
    n,
    wo_ref,
    mf_ref,
    mt_ref,
    q_ref,
    kv_ref,
    store_ref,
    out_ref,
    halo,
    mem_out,
    mem_in,
    req_out,
    req_in,
    req_now,
    bias,
    req_send,
    req_recv,
    local_sem,
    halo_send,
    halo_recv,
    mem_send,
    mem_recv,
):
    me = lax.axis_index("tile")
    heads = kv_ref.shape[0]
    frames = q_ref.shape[0]
    rows = TPD * TILE_TOK
    tokens = frames * rows
    listed = mt_ref.shape[1]
    per = heads // CHUNKS

    def peer_of(k):
        return lax.rem(me + k, n)

    barrier = pltpu.get_barrier_semaphore()

    @pl.loop(1, n)
    def _(k):
        pl.semaphore_signal(barrier, inc=1, device_id={"tile": peer_of(k)})

    row = lax.broadcasted_iota(jnp.int32, (n, 1, 128), 0)
    wanted = jnp.zeros((n, 1, 128), jnp.int32)
    for a in range(TPD):
        for j in range(listed):
            tile = mt_ref[a, j]
            slot = mf_ref[a, j] * TPD + lax.rem(tile, TPD)
            wanted = jnp.where(row == lax.div(tile, TPD), slot, wanted)
    req_out[...] = wanted

    pl.semaphore_wait(barrier, n - 1)

    def req_copy(k):
        return pltpu.make_async_remote_copy(
            src_ref=req_out.at[peer_of(k)],
            dst_ref=req_in.at[me],
            send_sem=req_send,
            recv_sem=req_recv,
            device_id={"tile": peer_of(k)},
        )

    @pl.loop(1, n)
    def _(k):
        req_copy(k).start()

    def halo_copy(side, c):
        part = pl.ds(c * per, per)
        return pltpu.make_async_remote_copy(
            src_ref=kv_ref.at[part],
            dst_ref=halo.at[side, part],
            send_sem=halo_send.at[side, c],
            recv_sem=halo_recv.at[side, c],
            device_id={"tile": lax.rem(me + 1, n) if side == 0 else lax.rem(me + n - 1, n)},
        )

    def send_halo(c):
        @pl.when(me < n - 1)
        def _():
            halo_copy(0, c).start()

        @pl.when(me > 0)
        def _():
            halo_copy(1, c).start()

    send_halo(0)

    column = lax.broadcasted_iota(jnp.int32, (TILE_TOK, 3 * tokens), 1)
    source = lax.div(column, tokens)
    local = lax.div(lax.rem(column, rows), TILE_TOK)
    span = local + jnp.where(source == 0, 0, jnp.where(source == 1, -TPD, TPD))
    there = span + me * TPD
    inside = (there >= 0) & (there < n * TPD)
    owner = lax.div(lax.broadcasted_iota(jnp.int32, (TILE_TOK, n * TILE_TOK), 1), TILE_TOK)
    for a in range(TPD):
        hit = jnp.zeros(span.shape, jnp.int32)
        for j in range(wo_ref.shape[0]):
            hit = jnp.where(span - a == wo_ref[j], 1, hit)
        near = jnp.where((hit == 1) & inside, 0.0, OFF)
        got = jnp.zeros(owner.shape, jnp.int32)
        for j in range(listed):
            got = jnp.where(owner == lax.div(mt_ref[a, j], TPD), 1, got)
        far = jnp.where(got == 1, 0.0, OFF)
        for f in range(frames):
            at = pl.ds(f * rows + a * TILE_TOK, TILE_TOK)
            bias[at, : 3 * tokens] = near
            bias[at, 3 * tokens :] = far

    @pl.when(me == 0)
    def _():
        @pl.loop(0, heads)
        def _(h):
            halo[0, h] = jnp.zeros(halo.shape[2:], halo.dtype)

    @pl.when(me == n - 1)
    def _():
        @pl.loop(0, heads)
        def _(h):
            halo[1, h] = jnp.zeros(halo.shape[2:], halo.dtype)

    pltpu.make_async_copy(
        req_in.at[pl.ds(0, n - 1)], req_in.at[pl.ds(0, n - 1)], req_recv
    ).wait()
    req_in[me] = req_out[me]
    to_scalar = pltpu.make_async_copy(req_in, req_now, local_sem)
    to_scalar.start()
    to_scalar.wait()

    def mem_copy(k, c):
        part = pl.ds(c * per, per)
        return pltpu.make_async_remote_copy(
            src_ref=mem_out.at[peer_of(k), part],
            dst_ref=mem_in.at[me, part],
            send_sem=mem_send,
            recv_sem=mem_recv.at[c],
            device_id={"tile": peer_of(k)},
        )

    for c in range(CHUNKS):
        part = pl.ds(c * per, per)
        if c > 0:
            send_halo(c)

        @pl.loop(1, n)
        def _(k):
            mem_out[peer_of(k), part] = store_ref[req_now[peer_of(k), 0, 0], part]
            mem_copy(k, c).start()

        mem_in[me, part] = store_ref[req_now[me, 0, 0], part]

    scale = HEAD_DIM**-0.5

    def one_head(h):
        at = pl.ds(pl.multiple_of(h * HEAD_DIM, HEAD_DIM), HEAD_DIM)
        q = q_ref[:, :, at].reshape(tokens, HEAD_DIM)
        pairs = [
            (kv_ref[h, 0], kv_ref[h, 1]),
            (halo[0, h, 0], halo[0, h, 1]),
            (halo[1, h, 0], halo[1, h, 1]),
            (
                mem_in[:, h, 0].reshape(n * TILE_TOK, HEAD_DIM),
                mem_in[:, h, 1].reshape(n * TILE_TOK, HEAD_DIM),
            ),
        ]
        keys = jnp.concatenate([k for k, _ in pairs], axis=0)
        values = jnp.concatenate([v for _, v in pairs], axis=0)
        scores = lax.dot_general(
            q, keys, (((1,), (1,)), ((), ())), preferred_element_type=jnp.float32
        )
        scores = scores * scale + bias[...]
        top = jnp.max(scores, axis=1, keepdims=True)
        terms = jnp.exp(scores - top)
        total = jnp.sum(terms, axis=1, keepdims=True)
        summed = jnp.dot(terms.astype(jnp.bfloat16), values, preferred_element_type=jnp.float32)
        out_ref[:, :, at] = (summed / total).astype(out_ref.dtype).reshape(frames, rows, HEAD_DIM)

    for c in range(CHUNKS):
        part = pl.ds(c * per, per)

        @pl.when(me > 0)
        def _():
            halo_copy(0, c).wait_recv()

        @pl.when(me < n - 1)
        def _():
            halo_copy(1, c).wait_recv()

        arrived = mem_in.at[pl.ds(0, n - 1), part]
        pltpu.make_async_copy(arrived, arrived, mem_recv.at[c]).wait()

        @pl.loop(c * per, (c + 1) * per)
        def _(h):
            one_head(h)

    for c in range(CHUNKS):

        @pl.when(me < n - 1)
        def _():
            halo_copy(0, c).wait_send()

        @pl.when(me > 0)
        def _():
            halo_copy(1, c).wait_send()

    gone = mem_out.at[pl.ds(0, n - 1)]
    pltpu.make_async_copy(gone, gone, mem_send).wait()
    pltpu.make_async_copy(
        req_out.at[pl.ds(0, n - 1)], req_out.at[pl.ds(0, n - 1)], req_send
    ).wait()


def body(queries, frame_kv, memory_kv, window_offsets, memory_frame, memory_tile):
    frames, rows, columns = queries.shape
    heads = columns // HEAD_DIM
    stored = memory_kv.shape[0]
    n = lax.axis_size("tile")
    kv = jnp.transpose(frame_kv.reshape(frames, rows, 2, heads, HEAD_DIM), (3, 2, 0, 1, 4))
    kv = kv.reshape(heads, 2, frames * rows, HEAD_DIM)
    store = jnp.transpose(
        memory_kv.reshape(stored * TPD, TILE_TOK, 2, heads, HEAD_DIM), (0, 3, 2, 1, 4)
    )
    tokens = frames * rows
    keys = 3 * tokens + n * TILE_TOK
    vmem = pl.BlockSpec(memory_space=pltpu.VMEM)
    smem = pl.BlockSpec(memory_space=pltpu.SMEM)
    dma = pltpu.SemaphoreType.DMA
    return pl.pallas_call(
        functools.partial(kernel, n),
        out_shape=jax.ShapeDtypeStruct(queries.shape, queries.dtype),
        in_specs=[smem, smem, smem, vmem, vmem, vmem],
        out_specs=vmem,
        scratch_shapes=[
            pltpu.VMEM((2, heads, 2, tokens, HEAD_DIM), jnp.bfloat16),
            pltpu.VMEM((n, heads, 2, TILE_TOK, HEAD_DIM), jnp.bfloat16),
            pltpu.VMEM((n, heads, 2, TILE_TOK, HEAD_DIM), jnp.bfloat16),
            pltpu.VMEM((n, 1, 128), jnp.int32),
            pltpu.VMEM((n, 1, 128), jnp.int32),
            pltpu.SMEM((n, 1, 128), jnp.int32),
            pltpu.VMEM((tokens, keys), jnp.float32),
            dma,
            dma,
            dma,
            dma((2, CHUNKS)),
            dma((2, CHUNKS)),
            dma,
            dma((CHUNKS,)),
        ],
        compiler_params=pltpu.CompilerParams(
            collective_id=0, has_side_effects=True, vmem_limit_bytes=56 * 2**20
        ),
        cost_estimate=pl.CostEstimate(
            flops=4 * tokens * keys * columns,
            bytes_accessed=12 * tokens * columns,
            transcendentals=tokens * keys * heads,
        ),
    )(window_offsets, memory_frame, memory_tile, queries, kv, store)


def solution(mesh):
    in_specs = (
        P("groups", "tile", None),
        P("groups", "tile", None, None),
        P("groups", "tile", None, None),
        P("groups"),
        P(("groups", "tile"), None),
        P(("groups", "tile"), None),
    )
    out_specs = P("groups", "tile", None)
    return jax.shard_map(body, mesh=mesh, in_specs=in_specs, out_specs=out_specs, check_vma=False)
```

time: 280 us -> 105 us (0.38); the launches traced: 275 us -> 105 us
  Pallas kernels: 0 us -> 89.3 us
  matrix products: 88.8 us -> 0 us
  local copies, waits for them, and re-layouts: 90.5 us -> 15.3 us
  other arithmetic: 47.5 us -> 0 us
  starting transfers between devices: 33.9 us -> 0 us
  waiting for transfers between devices: 12.8 us -> 0 us
    pallas_call x0 -> x1, Pallas kernels: none -> 89.3 us  [body(): pl.pallas_call(functools.partial(kernel, n), out_shape=jax.ShapeDtypeStru...]
    dot_general x16 -> x0, matrix products: 88.8 us -> none  [the longest x4 59.3 us: body(): jnp.einsum('fathd,gskhd->ahftgsk', query_part, near_keys, preferred_eleme...]
    another operation x16 -> x0, local copies, waits for them, and re-layouts: 35.8 us -> none  [the longest x4 10.7 us: body(): ext_tiles[..., 1, low:high]]
    reduce_sum x5 -> x0, other arithmetic: 32 us -> none  [body(): row_total = jnp.sum(near_terms, axis=(4, 5, 6)) + jnp.sum(far_terms, axis=4)]
    all_to_all x2 -> x0, starting transfers between devices: 28.9 us -> none  [the longest x1 20.9 us: body(): lax.all_to_all(picked, 'tile', split_axis=0, concat_axis=0, tiled=True)]
    gather x3 -> x0, local copies, waits for them, and re-layouts: 18 us -> none  [the longest x2 11 us: body(): fetched[owners.reshape(-1)].reshape(TPD, list_length * TILE_TOK, 2, columns)]
    concatenate x2 -> x0, other arithmetic: 13.5 us -> none  [the longest x1 11.4 us: with_halo(): array = jnp.concatenate([before, array, after], axis=dim)]
    all_to_all x2 -> x0, waiting for transfers between devices: 12.8 us -> none  [the longest x1 12.8 us: body(): lax.all_to_all(outgoing.reshape(peer_count, 1), 'tile', split_axis=0, con...]
  transfers between devices with their start and end apart: 4 -> 0, of which waited for: 1 -> 0; matrix products, arithmetic and copies ran while one was open for 36% -> 0% of each run, Pallas kernels for 0% -> 0%
where the time goes in v1:
time: 105 us
  Pallas kernels  89.3 us (85%)
  local copies, waits for them, and re-layouts  15.3 us (15%)
    pallas_call x1, Pallas kernels, body(): pl.pallas_call(functools.partial(kernel, n), out_shape=jax.ShapeDtypeStru...  89.3 us
    reshape x2, local copies, waits for them, and re-layouts, body(): memory_kv.reshape(stored * TPD, TILE_TOK, 2, heads, HEAD_DIM)  6.56 us
    reshape x1, local copies, waits for them, and re-layouts, body(): frame_kv.reshape(frames, rows, 2, heads, HEAD_DIM)  4.77 us
    unnamed x1, local copies, waits for them, and re-layouts  2.21 us

profile of v1, /device:TPU:0, one launch (start us, length us, event | category | flops | bytes accessed | tf_op | source)
XLA Modules:
  0.0 104.7 jit_solution(1392434426805483980)
XLA Ops:
  0.0 4.8 %reshape.12 = bf16[4,48,2,20,128]{4,3,2,1,0:T(8,128)(2,1)S(1)} reshape(bf16[4,48,2,2560]{3,2,1,0:T(2,128)(2,1)} %param.7) | data formatting | bytes 3932160 | tf_op jit(solution)/shard_map/reshape | solution.py:233
  4.8 1.8 %copy.9 = bf16[20,2,4,48,128]{4,3,2,1,0:T(8,128)(2,1)} copy(bf16[20,2,4,48,128]{4,0,1,3,2:T(8,128)(2,1)S(1)} %bitcast.6) | data formatting | bytes 3932160 | tf_op jit(solution)/shard_map/transpose | solution.py:233
  6.6 4.8 %reshape.13 = bf16[12,16,2,20,128]{4,3,2,1,0:T(8,128)(2,1)S(1)} reshape(bf16[4,48,2,2560]{3,2,1,0:T(2,128)(2,1)} %param.8) | data formatting | bytes 3932160 | tf_op jit(solution)/shard_map/reshape | solution.py:236
  11.4 1.8 %copy.17 = bf16[12,16,2,20,128]{4,1,2,3,0:T(8,128)(2,1)} copy(bf16[12,16,2,20,128]{4,3,2,1,0:T(8,128)(2,1)S(1)} %reshape.13) | data formatting | bytes 3932160 | tf_op jit(solution)/shard_map/reshape | solution.py:236
  13.1 89.3 %shard_map.64 = bf16[4,48,2560]{2,1,0:T(8,128)(2,1)} custom-call(s32[5]{0:T(128)} %wo_ref.1, s32[3,5]{1,0:T(4,128)} %mf_ref.1, s32[3,5]{1,0:T(4,128)} %mt_ref.1, bf16[4,48,2560]{2,1,0:T(8,128)(2,1)} %q_ref.1, bf16[20,2,192,128]{3,2,1,0:T(8,128)(2,1)} %bitcast.7, bf16[12,20,2,16,128]{4,3,2,1,0:T(8,128)(2,1)} %bitcast.8), custom_call_target="tpu_custom_call" | custom-call | flops 1635778560 | bytes 5898240 | tf_op jit(solution)/shard_map/pallas_call | solution.py:243
  102.5 2.2 %copy.19 = bf16[4,48,2560]{2,1,0:T(8,128)(2,1)} copy(bf16[4,48,2560]{2,1,0:T(8,128)(2,1)} %shard_map.64) | data formatting | bytes 1966080

commit v2 on v1

--- a/solution.py
+++ b/solution.py
@@ -20,10 +20,14 @@
     wo_ref,
     mf_ref,
     mt_ref,
+    q_hbm,
+    kv_hbm,
+    store_hbm,
+    out_hbm,
     q_ref,
-    kv_ref,
-    store_ref,
     out_ref,
+    own,
+    store,
     halo,
     mem_out,
     mem_in,
@@ -34,21 +38,28 @@
     req_send,
     req_recv,
     local_sem,
+    out_sem,
     halo_send,
     halo_recv,
     mem_send,
     mem_recv,
 ):
     me = lax.axis_index("tile")
-    heads = kv_ref.shape[0]
+    tokens, heads = kv_hbm.shape[:2]
     frames = q_ref.shape[0]
     rows = TPD * TILE_TOK
-    tokens = frames * rows
     listed = mt_ref.shape[1]
     per = heads // CHUNKS
 
     def peer_of(k):
         return lax.rem(me + k, n)
+
+    load_store = pltpu.make_async_copy(store_hbm, store, local_sem.at[0])
+    load_own = pltpu.make_async_copy(kv_hbm, own, local_sem.at[1])
+    load_q = pltpu.make_async_copy(q_hbm, q_ref, local_sem.at[2])
+    load_store.start()
+    load_own.start()
+    load_q.start()
 
     barrier = pltpu.get_barrier_semaphore()
 
@@ -81,10 +92,9 @@
         req_copy(k).start()
 
     def halo_copy(side, c):
-        part = pl.ds(c * per, per)
         return pltpu.make_async_remote_copy(
-            src_ref=kv_ref.at[part],
-            dst_ref=halo.at[side, part],
+            src_ref=kv_hbm.at[:, pl.ds(c * per, per)],
+            dst_ref=halo.at[side, c],
             send_sem=halo_send.at[side, c],
             recv_sem=halo_recv.at[side, c],
             device_id={"tile": lax.rem(me + 1, n) if side == 0 else lax.rem(me + n - 1, n)},
@@ -122,31 +132,19 @@
             bias[at, : 3 * tokens] = near
             bias[at, 3 * tokens :] = far
 
-    @pl.when(me == 0)
-    def _():
-        @pl.loop(0, heads)
-        def _(h):
-            halo[0, h] = jnp.zeros(halo.shape[2:], halo.dtype)
-
-    @pl.when(me == n - 1)
-    def _():
-        @pl.loop(0, heads)
-        def _(h):
-            halo[1, h] = jnp.zeros(halo.shape[2:], halo.dtype)
-
+    load_store.wait()
     pltpu.make_async_copy(
         req_in.at[pl.ds(0, n - 1)], req_in.at[pl.ds(0, n - 1)], req_recv
     ).wait()
     req_in[me] = req_out[me]
-    to_scalar = pltpu.make_async_copy(req_in, req_now, local_sem)
+    to_scalar = pltpu.make_async_copy(req_in, req_now, local_sem.at[3])
     to_scalar.start()
     to_scalar.wait()
 
     def mem_copy(k, c):
-        part = pl.ds(c * per, per)
         return pltpu.make_async_remote_copy(
-            src_ref=mem_out.at[peer_of(k), part],
-            dst_ref=mem_in.at[me, part],
+            src_ref=mem_out.at[c, peer_of(k)],
+            dst_ref=mem_in.at[c, me],
             send_sem=mem_send,
             recv_sem=mem_recv.at[c],
             device_id={"tile": peer_of(k)},
@@ -159,27 +157,40 @@
 
         @pl.loop(1, n)
         def _(k):
-            mem_out[peer_of(k), part] = store_ref[req_now[peer_of(k), 0, 0], part]
+            mem_out[c, peer_of(k)] = store[req_now[peer_of(k), 0, 0], :, part]
             mem_copy(k, c).start()
 
-        mem_in[me, part] = store_ref[req_now[me, 0, 0], part]
-
+        mem_in[c, me] = store[req_now[me, 0, 0], :, part]
+
+    @pl.when(me == 0)
+    def _():
+        @pl.loop(0, CHUNKS)
+        def _(c):
+            halo[0, c] = jnp.zeros(halo.shape[2:], halo.dtype)
+
+    @pl.when(me == n - 1)
+    def _():
+        @pl.loop(0, CHUNKS)
+        def _(c):
+            halo[1, c] = jnp.zeros(halo.shape[2:], halo.dtype)
+
+    load_own.wait()
+    load_q.wait()
     scale = HEAD_DIM**-0.5
 
-    def one_head(h):
+    def one_head(c, i):
+        h = c * per + i
         at = pl.ds(pl.multiple_of(h * HEAD_DIM, HEAD_DIM), HEAD_DIM)
         q = q_ref[:, :, at].reshape(tokens, HEAD_DIM)
         pairs = [
-            (kv_ref[h, 0], kv_ref[h, 1]),
-            (halo[0, h, 0], halo[0, h, 1]),
-            (halo[1, h, 0], halo[1, h, 1]),
-            (
-                mem_in[:, h, 0].reshape(n * TILE_TOK, HEAD_DIM),
-                mem_in[:, h, 1].reshape(n * TILE_TOK, HEAD_DIM),
-            ),
+            own[:, h],
+            halo[0, c, :, i],
+            halo[1, c, :, i],
+            mem_in[c, :, :, i].reshape(n * TILE_TOK, 2, HEAD_DIM),
         ]
-        keys = jnp.concatenate([k for k, _ in pairs], axis=0)
-        values = jnp.concatenate([v for _, v in pairs], axis=0)
+        pairs = [jnp.swapaxes(p, 0, 1) for p in pairs]
+        keys = jnp.concatenate([p[0] for p in pairs], axis=0)
+        values = jnp.concatenate([p[1] for p in pairs], axis=0)
         scores = lax.dot_general(
             q, keys, (((1,), (1,)), ((), ())), preferred_element_type=jnp.float32
         )
@@ -190,8 +201,11 @@
         summed = jnp.dot(terms.astype(jnp.bfloat16), values, preferred_element_type=jnp.float32)
         out_ref[:, :, at] = (summed / total).astype(out_ref.dtype).reshape(frames, rows, HEAD_DIM)
 
+    def out_copy(c):
+        at = pl.ds(c * per * HEAD_DIM, per * HEAD_DIM)
+        return pltpu.make_async_copy(out_ref.at[:, :, at], out_hbm.at[:, :, at], out_sem.at[c])
+
     for c in range(CHUNKS):
-        part = pl.ds(c * per, per)
 
         @pl.when(me > 0)
         def _():
@@ -201,12 +215,14 @@
         def _():
             halo_copy(1, c).wait_recv()
 
-        arrived = mem_in.at[pl.ds(0, n - 1), part]
+        arrived = mem_in.at[c, pl.ds(0, n - 1)]
         pltpu.make_async_copy(arrived, arrived, mem_recv.at[c]).wait()
 
-        @pl.loop(c * per, (c + 1) * per)
-        def _(h):
-            one_head(h)
+        @pl.loop(0, per)
+        def _(i):
+            one_head(c, i)
+
+        out_copy(c).start()
 
     for c in range(CHUNKS):
 
@@ -218,44 +234,50 @@
         def _():
             halo_copy(1, c).wait_send()
 
-    gone = mem_out.at[pl.ds(0, n - 1)]
+    gone = mem_out.at[:, pl.ds(0, n - 1)]
     pltpu.make_async_copy(gone, gone, mem_send).wait()
     pltpu.make_async_copy(
         req_out.at[pl.ds(0, n - 1)], req_out.at[pl.ds(0, n - 1)], req_send
     ).wait()
+    for c in range(CHUNKS):
+        out_copy(c).wait()
 
 
 def body(queries, frame_kv, memory_kv, window_offsets, memory_frame, memory_tile):
     frames, rows, columns = queries.shape
     heads = columns // HEAD_DIM
-    stored = memory_kv.shape[0]
+    stored = memory_kv.shape[0] * TPD
     n = lax.axis_size("tile")
-    kv = jnp.transpose(frame_kv.reshape(frames, rows, 2, heads, HEAD_DIM), (3, 2, 0, 1, 4))
-    kv = kv.reshape(heads, 2, frames * rows, HEAD_DIM)
-    store = jnp.transpose(
-        memory_kv.reshape(stored * TPD, TILE_TOK, 2, heads, HEAD_DIM), (0, 3, 2, 1, 4)
-    )
     tokens = frames * rows
     keys = 3 * tokens + n * TILE_TOK
-    vmem = pl.BlockSpec(memory_space=pltpu.VMEM)
+    kv = jnp.swapaxes(frame_kv.reshape(tokens, 2, heads, HEAD_DIM), 1, 2)
+    store = jnp.swapaxes(memory_kv.reshape(stored, TILE_TOK, 2, heads, HEAD_DIM), 2, 3)
+    anywhere = pl.BlockSpec(memory_space=pl.ANY)
     smem = pl.BlockSpec(memory_space=pltpu.SMEM)
     dma = pltpu.SemaphoreType.DMA
+    per = heads // CHUNKS
+    kept = jnp.bfloat16
     return pl.pallas_call(
         functools.partial(kernel, n),
         out_shape=jax.ShapeDtypeStruct(queries.shape, queries.dtype),
-        in_specs=[smem, smem, smem, vmem, vmem, vmem],
-        out_specs=vmem,
+        in_specs=[smem, smem, smem, anywhere, anywhere, anywhere],
+        out_specs=anywhere,
         scratch_shapes=[
-            pltpu.VMEM((2, heads, 2, tokens, HEAD_DIM), jnp.bfloat16),
-            pltpu.VMEM((n, heads, 2, TILE_TOK, HEAD_DIM), jnp.bfloat16),
-            pltpu.VMEM((n, heads, 2, TILE_TOK, HEAD_DIM), jnp.bfloat16),
+            pltpu.VMEM(queries.shape, kept),
+            pltpu.VMEM(queries.shape, kept),
+            pltpu.VMEM(kv.shape, kept),
+            pltpu.VMEM(store.shape, kept),
+            pltpu.VMEM((2, CHUNKS, tokens, per, 2, HEAD_DIM), kept),
+            pltpu.VMEM((CHUNKS, n, TILE_TOK, per, 2, HEAD_DIM), kept),
+            pltpu.VMEM((CHUNKS, n, TILE_TOK, per, 2, HEAD_DIM), kept),
             pltpu.VMEM((n, 1, 128), jnp.int32),
             pltpu.VMEM((n, 1, 128), jnp.int32),
             pltpu.SMEM((n, 1, 128), jnp.int32),
             pltpu.VMEM((tokens, keys), jnp.float32),
             dma,
             dma,
-            dma,
+            dma((4,)),
+            dma((CHUNKS,)),
             dma((2, CHUNKS)),
             dma((2, CHUNKS)),
             dma,

time: 105 us -> 91.1 us (0.87)
  local copies, waits for them, and re-layouts: 15.3 us -> 2.21 us
    reshape x3 -> x0, local copies, waits for them, and re-layouts: 11.3 us -> none  [the longest x2 6.56 us: body(): memory_kv.reshape(stored * TPD, TILE_TOK, 2, heads, HEAD_DIM)]
    transpose x1 -> x0, local copies, waits for them, and re-layouts: 1.79 us -> none  [body(): jnp.transpose(frame_kv.reshape(frames, rows, 2, heads, HEAD_DIM), (3, 2,...]
where the time goes in v2:
time: 91.1 us; the launch traced here: 90.9 us
  Pallas kernels  88.7 us (97%)
  local copies, waits for them, and re-layouts  2.21 us (2%)
    pallas_call x1, Pallas kernels, body(): pl.pallas_call(functools.partial(kernel, n), out_shape=jax.ShapeDtypeStru...  88.7 us
    unnamed x1, local copies, waits for them, and re-layouts  2.21 us

profile of v2, /device:TPU:0, one launch (start us, length us, event | category | flops | bytes accessed | tf_op | source)
XLA Modules:
  0.0 90.9 jit_solution(11587415907332407850)
XLA Ops:
  0.0 88.7 %shard_map.64 = bf16[4,48,2560]{2,1,0:T(8,128)(2,1)} custom-call(s32[5]{0:T(128)} %wo_ref.1, s32[3,5]{1,0:T(4,128)} %mf_ref.1, s32[3,5]{1,0:T(4,128)} %mt_ref.1, bf16[4,48,2560]{2,1,0:T(8,128)(2,1)} %q_hbm.1, bf16[192,20,2,128]{3,2,1,0:T(2,128)(2,1)} %bitcast.6, bf16[12,16,20,2,128]{4,3,2,1,0:T(2,128)(2,1)} %bitcast.7), custom_call_target="tpu_custom_call" | custom-call | flops 1635778560 | bytes 5898240 | tf_op jit(solution)/shard_map/pallas_call | solution.py:260
  88.7 2.2 %copy.8 = bf16[4,48,2560]{2,1,0:T(8,128)(2,1)} copy(bf16[4,48,2560]{2,1,0:T(8,128)(2,1)} %shard_map.64) | data formatting | bytes 1966080

commit v3 on v2

--- a/solution.py
+++ b/solution.py
@@ -12,11 +12,13 @@
 TPD = 3
 RADIUS = 3
 CHUNKS = 5
+LEAD = 2
 OFF = -1e30
 
 
 def kernel(
     n,
+    cornered,
     wo_ref,
     mf_ref,
     mt_ref,
@@ -29,6 +31,7 @@
     own,
     store,
     halo,
+    relay,
     mem_out,
     mem_in,
     req_out,
@@ -41,13 +44,14 @@
     out_sem,
     halo_send,
     halo_recv,
+    relay_recv,
+    relay_send,
     mem_send,
     mem_recv,
 ):
     me = lax.axis_index("tile")
-    tokens, heads = kv_hbm.shape[:2]
-    frames = q_ref.shape[0]
-    rows = TPD * TILE_TOK
+    frames, rows, heads = kv_hbm.shape[:3]
+    tokens = frames * rows
     listed = mt_ref.shape[1]
     per = heads // CHUNKS
 
@@ -91,25 +95,64 @@
     def _(k):
         req_copy(k).start()
 
-    def halo_copy(side, c):
+    exists = (me < n - 1, me > 0)
+    missing = (me == 0, me == n - 1)
+    level, place, levels = lax.div(me, 4), lax.rem(me, 4), n // 4
+    relayed = (lax.div(frames * (levels - 1 - level), levels), lax.div(frames * level, levels))
+    round_corner = (place == 3, place == 0)
+    is_relay = ((place == 0) & (me + 4 < n), (place == 3) & (me >= 4))
+
+    def halo_copy(side, c, f, by_relay):
+        to = (-3 if by_relay else 1) * (1 if side == 0 else -1)
         return pltpu.make_async_remote_copy(
-            src_ref=kv_hbm.at[:, pl.ds(c * per, per)],
-            dst_ref=halo.at[side, c],
-            send_sem=halo_send.at[side, c],
+            src_ref=kv_hbm.at[f, :, pl.ds(c * per, per)],
+            dst_ref=relay.at[c, f] if by_relay else halo.at[side, c, f],
+            send_sem=halo_send.at[side],
+            recv_sem=relay_recv.at[c, f] if by_relay else halo_recv.at[side, c],
+            device_id={"tile": lax.rem(me + to + n, n)},
+        )
+
+    def forward_copy(side, c, f):
+        return pltpu.make_async_remote_copy(
+            src_ref=relay.at[c, f],
+            dst_ref=halo.at[side, c, f],
+            send_sem=relay_send.at[c, f],
             recv_sem=halo_recv.at[side, c],
-            device_id={"tile": lax.rem(me + 1, n) if side == 0 else lax.rem(me + n - 1, n)},
-        )
-
-    def send_halo(c):
-        @pl.when(me < n - 1)
-        def _():
-            halo_copy(0, c).start()
-
-        @pl.when(me > 0)
-        def _():
-            halo_copy(1, c).start()
-
-    send_halo(0)
+            device_id={"tile": lax.rem(me + (4 if side == 0 else -4) + n, n)},
+        )
+
+    def send_halo(c, by_relay):
+        for side in range(2):
+            for f in range(frames):
+                if not cornered:
+                    go = None if by_relay else exists[side]
+                else:
+                    via = round_corner[side] & (f < relayed[side])
+                    go = exists[side] & (via if by_relay else ~via)
+                    if by_relay and f == frames - 1:
+                        go = None
+                if go is not None:
+
+                    @pl.when(go)
+                    def _():
+                        halo_copy(side, c, f, by_relay).start()
+
+    def at_relay(c, act):
+        if cornered:
+            for side in range(2):
+                for f in range(frames - 1):
+
+                    @pl.when(is_relay[side] & (f < relayed[side]))
+                    def _():
+                        act(side, c, f)
+
+    def forward(side, c, f):
+        halo_copy(side, c, f, True).wait_recv()
+        forward_copy(side, c, f).start()
+
+    for c in range(LEAD):
+        send_halo(c, True)
+    send_halo(0, False)
 
     column = lax.broadcasted_iota(jnp.int32, (TILE_TOK, 3 * tokens), 1)
     source = lax.div(column, tokens)
@@ -152,8 +195,10 @@
 
     for c in range(CHUNKS):
         part = pl.ds(c * per, per)
+        if c + LEAD < CHUNKS:
+            send_halo(c + LEAD, True)
         if c > 0:
-            send_halo(c)
+            send_halo(c, False)
 
         @pl.loop(1, n)
         def _(k):
@@ -162,18 +207,15 @@
 
         mem_in[c, me] = store[req_now[me, 0, 0], :, part]
 
-    @pl.when(me == 0)
-    def _():
-        @pl.loop(0, CHUNKS)
-        def _(c):
-            halo[0, c] = jnp.zeros(halo.shape[2:], halo.dtype)
-
-    @pl.when(me == n - 1)
-    def _():
-        @pl.loop(0, CHUNKS)
-        def _(c):
-            halo[1, c] = jnp.zeros(halo.shape[2:], halo.dtype)
-
+    for side in range(2):
+
+        @pl.when(missing[side])
+        def _():
+            @pl.loop(0, CHUNKS)
+            def _(c):
+                halo[side, c] = jnp.zeros(halo.shape[2:], halo.dtype)
+
+    at_relay(0, forward)
     load_own.wait()
     load_q.wait()
     scale = HEAD_DIM**-0.5
@@ -183,9 +225,9 @@
         at = pl.ds(pl.multiple_of(h * HEAD_DIM, HEAD_DIM), HEAD_DIM)
         q = q_ref[:, :, at].reshape(tokens, HEAD_DIM)
         pairs = [
-            own[:, h],
-            halo[0, c, :, i],
-            halo[1, c, :, i],
+            own[:, :, h].reshape(tokens, 2, HEAD_DIM),
+            halo[0, c, :, :, i].reshape(tokens, 2, HEAD_DIM),
+            halo[1, c, :, :, i].reshape(tokens, 2, HEAD_DIM),
             mem_in[c, :, :, i].reshape(n * TILE_TOK, 2, HEAD_DIM),
         ]
         pairs = [jnp.swapaxes(p, 0, 1) for p in pairs]
@@ -206,14 +248,15 @@
         return pltpu.make_async_copy(out_ref.at[:, :, at], out_hbm.at[:, :, at], out_sem.at[c])
 
     for c in range(CHUNKS):
-
-        @pl.when(me > 0)
-        def _():
-            halo_copy(0, c).wait_recv()
-
-        @pl.when(me < n - 1)
-        def _():
-            halo_copy(1, c).wait_recv()
+        if c + 1 < CHUNKS:
+            at_relay(c + 1, forward)
+
+        for side in range(2):
+
+            @pl.when(~missing[side])
+            def _():
+                arrived = halo.at[side, c]
+                pltpu.make_async_copy(arrived, arrived, halo_recv.at[side, c]).wait()
 
         arrived = mem_in.at[c, pl.ds(0, n - 1)]
         pltpu.make_async_copy(arrived, arrived, mem_recv.at[c]).wait()
@@ -224,16 +267,15 @@
 
         out_copy(c).start()
 
+    for side in range(2):
+
+        @pl.when(exists[side])
+        def _():
+            gone = halo.at[side]
+            pltpu.make_async_copy(gone, gone, halo_send.at[side]).wait()
+
     for c in range(CHUNKS):
-
-        @pl.when(me < n - 1)
-        def _():
-            halo_copy(0, c).wait_send()
-
-        @pl.when(me > 0)
-        def _():
-            halo_copy(1, c).wait_send()
-
+        at_relay(c, lambda side, c, f: forward_copy(side, c, f).wait_send())
     gone = mem_out.at[:, pl.ds(0, n - 1)]
     pltpu.make_async_copy(gone, gone, mem_send).wait()
     pltpu.make_async_copy(
@@ -243,14 +285,14 @@
         out_copy(c).wait()
 
 
-def body(queries, frame_kv, memory_kv, window_offsets, memory_frame, memory_tile):
+def body(cornered, queries, frame_kv, memory_kv, window_offsets, memory_frame, memory_tile):
     frames, rows, columns = queries.shape
     heads = columns // HEAD_DIM
     stored = memory_kv.shape[0] * TPD
     n = lax.axis_size("tile")
     tokens = frames * rows
     keys = 3 * tokens + n * TILE_TOK
-    kv = jnp.swapaxes(frame_kv.reshape(tokens, 2, heads, HEAD_DIM), 1, 2)
+    kv = jnp.swapaxes(frame_kv.reshape(frames, rows, 2, heads, HEAD_DIM), 2, 3)
     store = jnp.swapaxes(memory_kv.reshape(stored, TILE_TOK, 2, heads, HEAD_DIM), 2, 3)
     anywhere = pl.BlockSpec(memory_space=pl.ANY)
     smem = pl.BlockSpec(memory_space=pltpu.SMEM)
@@ -258,7 +300,7 @@
     per = heads // CHUNKS
     kept = jnp.bfloat16
     return pl.pallas_call(
-        functools.partial(kernel, n),
+        functools.partial(kernel, n, cornered),
         out_shape=jax.ShapeDtypeStruct(queries.shape, queries.dtype),
         in_specs=[smem, smem, smem, anywhere, anywhere, anywhere],
         out_specs=anywhere,
@@ -267,7 +309,8 @@
             pltpu.VMEM(queries.shape, kept),
             pltpu.VMEM(kv.shape, kept),
             pltpu.VMEM(store.shape, kept),
-            pltpu.VMEM((2, CHUNKS, tokens, per, 2, HEAD_DIM), kept),
+            pltpu.VMEM((2, CHUNKS, frames, rows, per, 2, HEAD_DIM), kept),
+            pltpu.VMEM((CHUNKS, frames - 1, rows, per, 2, HEAD_DIM), kept),
             pltpu.VMEM((CHUNKS, n, TILE_TOK, per, 2, HEAD_DIM), kept),
             pltpu.VMEM((CHUNKS, n, TILE_TOK, per, 2, HEAD_DIM), kept),
             pltpu.VMEM((n, 1, 128), jnp.int32),
@@ -278,8 +321,10 @@
             dma,
             dma((4,)),
             dma((CHUNKS,)),
+            dma((2,)),
             dma((2, CHUNKS)),
-            dma((2, CHUNKS)),
+            dma((CHUNKS, frames - 1)),
+            dma((CHUNKS, frames - 1)),
             dma,
             dma((CHUNKS,)),
         ],
@@ -294,6 +339,21 @@
     )(window_offsets, memory_frame, memory_tile, queries, kv, store)
 
 
+def has_corners(mesh):
+    line = mesh.devices[0]
+    if mesh.axis_names != ("groups", "tile") or len(line) % 4 or len(line) < 8:
+        return False
+    spots = [d.coords for d in line]
+
+    def apart(i, j):
+        return sum(p != q for p, q in zip(spots[i], spots[j]))
+
+    whole = range(0, len(line), 4)
+    return all(
+        apart(i, i + 1) == 0 and apart(i + 2, i + 3) == 0 and apart(i, i + 2) == 1 for i in whole
+    ) and all(apart(i - 1, i) == 2 and apart(i - 4, i) == 1 for i in whole[1:])
+
+
 def solution(mesh):
     in_specs = (
         P("groups", "tile", None),
@@ -304,4 +364,6 @@
         P(("groups", "tile"), None),
     )
     out_specs = P("groups", "tile", None)
-    return jax.shard_map(body, mesh=mesh, in_specs=in_specs, out_specs=out_specs, check_vma=False)
+    return jax.shard_map(
+        functools.partial(body, has_corners(mesh)), mesh=mesh, in_specs=in_specs, out_specs=out_specs, check_vma=False
+    )

time: 91.1 us -> 89.7 us (0.985)
  the two profiles are of different devices: /device:TPU:0 before, /device:TPU:13 now
where the time goes in v3:
time: 89.7 us; the launch traced here: 89.6 us
  Pallas kernels  87.4 us (97%)
  local copies, waits for them, and re-layouts  2.21 us (2%)
    pallas_call x1, Pallas kernels, body(): pl.pallas_call(functools.partial(kernel, n, cornered), out_shape=jax.Shap...  87.4 us
    unnamed x1, local copies, waits for them, and re-layouts  2.21 us

profile of v3, /device:TPU:13, one launch (start us, length us, event | category | flops | bytes accessed | tf_op | source)
XLA Modules:
  0.0 89.6 jit_solution(11132084206459906471)
XLA Ops:
  0.0 87.4 %shard_map.64 = bf16[4,48,2560]{2,1,0:T(8,128)(2,1)} custom-call(s32[5]{0:T(128)} %wo_ref.1, s32[3,5]{1,0:T(4,128)} %mf_ref.1, s32[3,5]{1,0:T(4,128)} %mt_ref.1, bf16[4,48,2560]{2,1,0:T(8,128)(2,1)} %q_hbm.1, bf16[4,48,20,2,128]{4,3,2,1,0:T(2,128)(2,1)} %bitcast.6, bf16[12,16,20,2,128]{4,3,2,1,0:T(2,128)(2,1)} %bitcast.7), custom_call_target="tpu_custom_call" | custom-call | flops 1635778560 | bytes 5898240 | tf_op jit(solution)/shard_map/pallas_call | solution.py:302
  87.4 2.2 %copy.8 = bf16[4,48,2560]{2,1,0:T(8,128)(2,1)} copy(bf16[4,48,2560]{2,1,0:T(8,128)(2,1)} %shard_map.64) | data formatting | bytes 1966080
